TPU v7x, 128 devices: a whole 4x4x4 slice. The times are simulated.
128 devices in a mesh: ctx: 8 (over x_hi, y), head: 8 (over z, core), var: 2 (over x_lo).
Axes of the slice: x: 4 (x_hi: 2, x_lo: 2; x = x_hi * 2 + x_lo), y: 4, z: 4, core: 2. Of those that a mesh axis runs over, the one named last changes fastest.
Arguments:
- sequence: bfloat16 [4096, 1536], P('ctx', 'head'), may hold values from -8 to 8
- deletions: int32 [8, 2], P('var'), parts along dimension 0, may hold values from 0 to 4096, as said below
- conv_taps: float32 [3, 1536], P(None, 'head'), may hold values from -3 to 3
- conv_bias: float32 [1536], P('head'), may hold values from -3 to 3
- w_proj: bfloat16 [1536, 3584], P(None, 'head'), may hold values from -1 to 1
- w_out: bfloat16 [1536, 1536], P('head'), may hold values from -0.15625 to 0.15625
- w_pair: bfloat16 [1536, 256], P('head'), may hold values from -0.15625 to 0.15625
- dist_table: float32 [16, 128], replicated, may hold values from -3 to 3
Outputs:
- pair_map: bfloat16 [8, 1024, 1024, 128], P('var', 'ctx', 'head'), parts along dimension 0
There are 2 independent parts, one for each index of `var`. A program takes and returns all parts, laid end to end along the dimension named above; an argument that names none is the same for every part. Nothing has to cross between parts.
Inputs may be any that keep to these rules, and one draw needn't show every extreme that they name: `deletions`: each variant deletes 1 to 128 consecutive tokens, some variant deletes exactly 128, and some variant's deletion ends at the last token of the locus.
All inputs are finite; a program needn't handle non-finite values.
Results may differ from a plain program's by a relative error of at most 0.025.
Values may be sent and summed in bfloat16 or wider, within the bound.
A program may use at most 128 MiB of HBM per device.

v0:
```python
import math
import jax
import jax.numpy as jnp
from jax import lax
from jax.sharding import PartitionSpec as P

HD = 128
VD = 192
C = 128
NB = 16
POOL = 4


def extended(block, sides, width):
    for axis, dim in sides:
        count = lax.axis_size(axis)
        forward = [(i, i + 1) for i in range(count - 1)]
        backward = [(target, source) for source, target in forward]
        low = lax.ppermute(
            lax.slice_in_dim(block, block.shape[dim] - width, None, axis=dim), axis, forward
        )
        high = lax.ppermute(lax.slice_in_dim(block, 0, width, axis=dim), axis, backward)
        block = jnp.concatenate([low, block, high], axis=dim)
    return block


def attend_block(running, queries, key_rows, value_rows):
    row_max, row_sum, weighted = running
    scores = jnp.einsum(
        "vqhe,vkhe->vhqk", queries, key_rows, preferred_element_type=jnp.float32
    ) / math.sqrt(queries.shape[-1])
    new_max = jnp.maximum(row_max, scores.max(-1))
    shrink = jnp.exp(row_max - new_max)
    weights = jnp.exp(scores - new_max[..., None])
    row_sum = row_sum * shrink + weights.sum(-1)
    weighted = weighted * shrink[..., None] + jnp.einsum(
        "vhqk,vkhe->vhqe",
        weights.astype(jnp.bfloat16),
        value_rows,
        preferred_element_type=jnp.float32,
    )
    return (new_max, row_sum, weighted)


def attend_rows(running, queries, key_rows, value_rows):
    key_total = key_rows.shape[1]
    block_rows = 512
    block_count = key_total // block_rows

    def block_step(block_index, state_now):
        key_part = lax.dynamic_slice_in_dim(key_rows, block_index * block_rows, block_rows, 1)
        value_part = lax.dynamic_slice_in_dim(value_rows, block_index * block_rows, block_rows, 1)
        return attend_block(state_now, queries, key_part, value_part)

    return lax.fori_loop(0, block_count, block_step, running)


def local(sequence, deletions, conv_taps, conv_bias, w_proj, w_out, w_pair, dist_table):
    token_count, local_width = sequence.shape
    variants = deletions.shape[0]
    head_count = w_out.shape[0] // VD
    row_start = lax.axis_index("ctx") * token_count
    positions = row_start + jnp.arange(token_count, dtype=jnp.int32)
    kept = jnp.logical_or(
        positions[None, :] < deletions[:, 0:1], positions[None, :] >= deletions[:, 1:2]
    )
    masked = jnp.where(kept[:, :, None], sequence[None], jnp.zeros((), jnp.bfloat16))
    dilation = token_count // 2
    padded = extended(masked, (("ctx", 1),), dilation)
    spread = padded.astype(jnp.float32)
    middle = spread[:, dilation : dilation + token_count]
    convolved = (
        conv_taps[0] * spread[:, :token_count]
        + conv_taps[1] * middle
        + conv_taps[2] * spread[:, 2 * dilation : 2 * dilation + token_count]
        + conv_bias
    )
    trunk_out = (middle + jax.nn.gelu(convolved, approximate=True)).astype(jnp.bfloat16)
    projected = jnp.einsum(
        "vtd,df->vtf",
        lax.all_gather(trunk_out, "head", axis=2, tiled=True),
        w_proj,
        preferred_element_type=jnp.float32,
    ).astype(jnp.bfloat16)
    projected = projected.reshape(trunk_out.shape[0], token_count, head_count, 2 * HD + VD)
    queries = projected[:variants, :, :, :HD]
    key_rows = projected[:, :, :, HD : 2 * HD]
    value_rows = projected[:, :, :, 2 * HD :]
    running = attend_rows(
        (
            jnp.full((variants, head_count, token_count), -jnp.inf, jnp.float32),
            jnp.zeros((variants, head_count, token_count), jnp.float32),
            jnp.zeros((variants, head_count, token_count, VD), jnp.float32),
        ),
        queries,
        lax.all_gather(key_rows, "ctx", axis=1, tiled=True),
        lax.all_gather(value_rows, "ctx", axis=1, tiled=True),
    )
    row_max, row_sum, weighted = running
    head_out = (weighted / row_sum[..., None]).astype(jnp.bfloat16)
    flat_out = head_out.transpose(0, 2, 1, 3).reshape(variants * token_count, head_count * VD)
    mixed_back = lax.psum_scatter(
        lax.dot_general(
            w_out, flat_out, (((0,), (1,)), ((), ())), preferred_element_type=jnp.float32
        ).astype(jnp.bfloat16),
        "head",
        scatter_dimension=0,
        tiled=True,
    ).astype(jnp.float32)
    residual = trunk_out.astype(jnp.float32) + mixed_back.T.reshape(
        variants, token_count, local_width
    )
    pooled = (
        residual.reshape(variants, token_count // POOL, POOL, local_width)
        .mean(2)
        .astype(jnp.bfloat16)
    )
    partial_value = jnp.einsum("vpd,dc->vpc", pooled, w_pair, preferred_element_type=jnp.float32)
    pair_proj = lax.psum(partial_value.astype(jnp.bfloat16), "head").astype(jnp.float32)
    row_feats = pair_proj[:, :, :C]
    all_cols = lax.all_gather(
        pair_proj[:, :, C:].astype(jnp.bfloat16), "ctx", axis=1, tiled=True
    ).astype(jnp.float32)
    col_count = all_cols.shape[1] // lax.axis_size("head")
    col_start = lax.axis_index("head") * col_count
    col_feats = lax.dynamic_slice_in_dim(all_cols, col_start, col_count, 1)
    row_ids = lax.axis_index("ctx") * (token_count // POOL) + jnp.arange(
        token_count // POOL, dtype=jnp.int32
    )
    col_ids = col_start + jnp.arange(col_count, dtype=jnp.int32)
    distance = jnp.abs(row_ids[:, None] - col_ids[None, :])
    buckets = jnp.zeros(distance.shape, jnp.int32)
    for power_index in range(NB - 1):
        buckets = buckets + (distance >= 2**power_index).astype(jnp.int32)
    one_hot = (buckets[:, :, None] == jnp.arange(NB, dtype=jnp.int32)).astype(jnp.float32)
    rel_table = jnp.dot(one_hot, dist_table, precision=lax.Precision.HIGHEST)
    pair_map = row_feats[:, :, None, :] + col_feats[:, None, :, :] + rel_table[None]
    return pair_map.astype(jnp.bfloat16)


def solution(mesh):
    in_specs = (
        P("ctx", "head"),
        P("var", None),
        P(None, "head"),
        P("head"),
        P(None, "head"),
        P("head", None),
        P("head", None),
        P(),
    )
    out_specs = P("var", "ctx", "head", None)
    return jax.shard_map(local, mesh=mesh, in_specs=in_specs, out_specs=out_specs, check_vma=False)
```

profile of v0, /device:TPU:0, one launch (start us, length us, event | category | flops | bytes accessed | tf_op | source)
XLA Modules:
  0.0 486.1 jit_solution(6132765217847577570)
XLA Ops:
  6.5 0.8 slice_bitcast_fusion.1
  7.4 1.0 broadcast_select_fusion
  8.5 3.6 collective-permute-start
  12.1 1.3 collective-permute-start.1
  13.4 7.0 %collective-permute-done = bf16[4,256,192]{1,2,0:T(8,128)(2,1)S(1)} collective-permute-done((bf16[4,256,192]{1,2,0:T(8,128)(2,1)S(1)}, bf16[4,256,192]{1,2,0:T(8,128)(2,1)S(1)}, u32[]{:S(2)}, u32[]{:S(2)}) %collective-permute-start) | collective-permute-done | bytes 393248 | tf_op jit(solution)/shard_map/ppermute | solution.py:19
  20.4 4.1 collective-permute-done.1
  25.0 1.8 copy-done.2
  26.8 2.0 fusion.28
  28.8 45.7 %all-gather.5.cloned.1.call-done = bf16[4,512,1536]{1,2,0:T(8,128)(2,1)} async-done(((bf16[4,512,192]{1,2,0:T(8,128)(2,1)}), bf16[4,512,1536]{1,2,0:T(8,128)(2,1)}) %all-gather.5.cloned.1.call-update) | async-done | bytes 6291472 | tf_op jit(solution)/shard_map/all_gather | solution.py:81
  74.5 5.8 %convert_bitcast_fusion = bf16[4,512,1,448]{1,3,0,2:T(8,128)(2,1)S(1)} fusion(bf16[4,512,1536]{1,2,0:T(8,128)(2,1)} %all-gather.5.cloned.1.call-done, bf16[1536,448]{0,1:T(8,128)(2,1)S(1)} %copy-done), kind=kOutput, calls=%fused_computation.29 | convolution fusion | flops 2819489792 | bytes 9502720 | tf_op jit(solution)/shard_map/vtd,df->vtf/dot_general | solution.py:79
  80.3 1.2 copy-done.4
  81.5 0.9 fusion.54
  82.5 2.1 slice.78
  85.0 71.1 %all-gather.7.cloned.1.call-done = bf16[4,4096,1,128]{1,3,0,2:T(8,128)(2,1)} async-done(((bf16[4,512,1,128]{1,3,0,2:T(8,128)(2,1)}), bf16[4,4096,1,128]{1,3,0,2:T(8,128)(2,1)}) %all-gather.7.cloned.1.call-update) | async-done | bytes 4194320 | tf_op jit(solution)/shard_map/all_gather | solution.py:96
  156.1 93.5 %all-gather.9.cloned.1.call-done = bf16[4,4096,1,192]{1,3,0,2:T(8,128)(2,1)} async-done(((bf16[4,512,1,192]{1,3,0,2:T(8,128)(2,1)}), bf16[4,4096,1,192]{1,3,0,2:T(8,128)(2,1)}) %all-gather.9.cloned.1.call-update) | async-done | bytes 6291472 | tf_op jit(solution)/shard_map/all_gather | solution.py:97
  249.6 40.1 %while.18 = (s32[]{:T(128)}, f32[4,1,512]{2,0,1:T(4,128)S(1)}, f32[4,1,512]{2,0,1:T(4,128)S(1)}, f32[4,1,512,192]{2,3,0,1:T(8,128)S(1)}, bf16[4,4096,1,128]{1,3,...) while((s32[]{:T(128)}, f32[4,1,512]{2,0,1:T(4,128)S(1)}, ...), condition=%wide.region_3.4_spmd.clone, body=%wide.region_0.3_spmd.clone.sunk | while | flops 680669184 | bytes 17694904 | solution.py:55
  249.6 1.8 bitcast_reduce_fusion.3
  252.1 2.4 bitcast_add_fusion.5
  254.6 1.8 bitcast_reduce_fusion.3
  257.1 2.4 bitcast_add_fusion.5
  259.6 1.8 bitcast_reduce_fusion.3
  261.5 0.7 fusion.67
  262.2 2.4 bitcast_add_fusion.5
  264.6 1.8 bitcast_reduce_fusion.3
  267.2 2.4 bitcast_add_fusion.5
  269.7 1.8 bitcast_reduce_fusion.3
  272.2 2.4 bitcast_add_fusion.5
  274.7 1.8 bitcast_reduce_fusion.3
  277.2 2.4 bitcast_add_fusion.5
  279.7 1.8 bitcast_reduce_fusion.3
  282.2 2.4 bitcast_add_fusion.5
  284.7 1.8 bitcast_reduce_fusion.3
  287.3 2.4 bitcast_add_fusion.5
  291.0 4.5 fusion.19
  295.6 8.7 %copy.38 = bf16[1536,2048]{1,0:T(8,128)(2,1)} copy(bf16[1536,2048]{0,1:T(8,128)(2,1)} %fusion.19) | data formatting | bytes 12582912
  304.5 40.6 %reduce-scatter.4.cloned.1.call-done = bf16[192,2048]{1,0:T(8,128)(2,1)} async-done(((bf16[1536,2048]{1,0:T(8,128)(2,1)}), bf16[192,2048]{1,0:T(8,128)(2,1)}) %reduce-scatter.4.cloned.1.call-update) | async-done | bytes 786448
  345.1 1.4 copy.39
  346.5 1.5 reshape.213
  348.0 2.9 copy.32
  351.0 3.6 convert_add_fusion
  354.6 2.0 copy.33
  357.5 1.0 convolution_convert_fusion.1
  358.5 59.7 %all-reduce.2.cloned.1.call-done = bf16[4,128,256]{2,1,0:T(8,128)(2,1)} async-done(((bf16[4,128,256]{2,1,0:T(8,128)(2,1)}), bf16[4,128,256]{2,1,0:T(8,128)(2,1)}) %all-reduce.2.cloned.1.call-update) | async-done | bytes 262160 | tf_op jit(solution)/shard_map/psum | solution.py:119
  418.2 1.6 slice_convert_fusion
  420.1 8.9 %fusion.33 = f32[128,128,128]{2,1,0:T(8,128)} fusion(s32[128,128]{1,0:T(8,128)S(1)} %convert_add_fusion.1, f32[16,128]{1,0:T(8,128)S(1)} %copy-done.7), kind=kOutput, calls=%fused_computation.50 | convolution fusion | flops 402915328 | bytes 8462336 | tf_op jit(solution)/shard_map/dot_general | solution.py:136
  429.0 36.8 %all-gather.11.cloned.1.call-done = bf16[4,1024,128]{2,1,0:T(8,128)(2,1)} async-done(((bf16[4,128,128]{2,1,0:T(8,128)(2,1)}), bf16[4,1024,128]{2,1,0:T(8,128)(2,1)}) %all-gather.11.cloned.1.call-update) | async-done | bytes 1048592 | tf_op jit(solution)/shard_map/all_gather | solution.py:121
  465.9 0.9 dynamic-slice_convert_fusion
  466.8 12.4 %add_convert_fusion = bf16[4,128,128,128]{3,2,1,0:T(8,128)(2,1)} fusion(f32[128,128,128]{2,1,0:T(8,128)} %fusion.33, f32[4,128,128]{2,1,0:T(8,128)S(1)} %dynamic-slice_convert_fusion, f32[4,128,128]{2,1,0:T(8,128)S(1)} %get-tuple-element.206), kind=kLoop, calls=%fused_computation.24 | loop fusion | flops 25165824 | bytes 25690112 | tf_op jit(solution)/shard_map/convert_element_type | solution.py:138
  (77 shorter events, 8.9 us)
Async XLA Ops:
  6.5 68.0 %copy-start = (bf16[1536,448]{0,1:T(8,128)(2,1)S(1)}, bf16[1536,448]{0,1:T(8,128)(2,1)}, u32[]{:S(2)}) copy-start(bf16[1536,448]{0,1:T(8,128)(2,1)} %param.14) | copy-start | bytes 4128772
  6.5 6.9 %copy-start.9 = (f32[3,192]{1,0:T(4,128)S(1)}, f32[3,192]{1,0:T(4,128)}, u32[]{:S(2)}) copy-start(f32[3,192]{1,0:T(4,128)} %param.12) | copy-start | bytes 6916
  6.5 68.0 %all-gather.5.cloned.1.call-start = ((), (), s32[]{:S(2)}) async-start(), calls=%async_computation.1 | async-start | bytes 7077888 | tf_op jit(solution)/shard_map/all_gather | solution.py:81
  8.5 11.9 %collective-permute-start = (bf16[4,256,192]{1,2,0:T(8,128)(2,1)S(1)}, bf16[4,256,192]{1,2,0:T(8,128)(2,1)S(1)}, u32[]{:S(2)}, u32[]{:S(2)}) collective-permute-start(bf16[4,256,192]{1,2,0:T(8,128)(2,1)S(1)} %get-tuple-element.204), channel_id=1, source_target_pairs={{0,16},{16,32},{32,48},{48,64},{64,80},{80,96},{96,112},{1,17},{17... | collective-permute-start | bytes 1179656 | tf_op jit(solution)/shard_map/ppermute | solution.py:19
  12.1 12.5 %collective-permute-start.1 = (bf16[4,256,192]{1,2,0:T(8,128)(2,1)S(1)}, bf16[4,256,192]{1,2,0:T(8,128)(2,1)S(1)}, u32[]{:S(2)}, u32[]{:S(2)}) collective-permute-start(bf16[4,256,192]{1,2,0:T(8,128)(2,1)S(1)} %get-tuple-element.205), channel_id=1, source_target_pairs={{16,0},{32,16},{48,32},{64,48},{80,64},{96,80},{112,96},{17,1},{33... | collective-permute-start | bytes 1179656 | tf_op jit(solution)/shard_map/ppermute | solution.py:22
  13.4 13.4 %copy-start.8 = (f32[192]{0:T(256)S(1)}, f32[192]{0:T(256)}, u32[]{:S(2)}) copy-start(f32[192]{0:T(256)} %param.13) | copy-start | bytes 2308
  25.0 1.8 copy-start.2
  28.8 127.3 %all-gather.7.cloned.1.call-start = ((), (), s32[]{:S(2)}) async-start(), calls=%async_computation.2 | async-start | bytes 4718592 | tf_op jit(solution)/shard_map/all_gather | solution.py:96
  80.3 1.2 copy-start.4
  82.4 167.1 %all-gather.9.cloned.1.call-start = ((), (), s32[]{:S(2)}) async-start(), calls=%async_computation.3 | async-start | bytes 7077888 | tf_op jit(solution)/shard_map/all_gather | solution.py:97
  84.6 260.5 %reduce-scatter.4.cloned.1.call-start = ((), (), s32[]{:S(2)}) async-start(), calls=%async_computation.6 | async-start | bytes 7077888
  289.9 1.1 copy-start.5
  304.3 113.9 %all-reduce.2.cloned.1.call-start = ((), (), s32[]{:S(2)}) async-start(), calls=%async_computation.4 | async-start | bytes 524288 | tf_op jit(solution)/shard_map/psum | solution.py:119
  348.0 2.9 copy-start.3
  356.6 0.9 copy-start.6
  357.2 63.0 %copy-start.7 = (f32[16,128]{1,0:T(8,128)S(1)}, f32[16,128]{1,0:T(8,128)}, u32[]{:S(2)}) copy-start(f32[16,128]{1,0:T(8,128)} %param.17) | copy-start | bytes 24580
  358.5 107.4 %all-gather.11.cloned.1.call-start = ((), (), s32[]{:S(2)}) async-start(), calls=%async_computation.5 | async-start | bytes 1179648 | tf_op jit(solution)/shard_map/all_gather | solution.py:121
  466.8 12.4 %copy-start.1 = (bf16[1536,448]{0,1:T(8,128)(2,1)S(1)}, bf16[1536,448]{0,1:T(8,128)(2,1)}, u32[]{:S(2)}) copy-start(bf16[1536,448]{0,1:T(8,128)(2,1)} %param.14) | copy-start | bytes 4128772
Sparse Core Ops, SparseCore 0:
  28.9 45.5 all-gather.4
  82.6 73.4 all-gather.6
  158.3 91.2 all-gather.8
  304.4 40.6 reduce-scatter.3
  358.6 59.6 all-reduce.1
  420.7 45.1 all-gather.10
where the time goes:
time: 488 us; the launch traced here: 486 us
  waiting for transfers between devices  359 us (74%)
  matrix products  54 us (11%)
  other arithmetic  30.4 us (6%)
  local copies, waits for them, and re-layouts  23.6 us (5%)
  between operations  13.7 us (3%)
  starting transfers between devices  5.27 us (1%)
    all_gather x1, waiting for transfers between devices, local(): lax.all_gather(value_rows, 'ctx', axis=1, tiled=True)  93.5 us
    all_gather x1, waiting for transfers between devices, local(): lax.all_gather(key_rows, 'ctx', axis=1, tiled=True)  71.1 us
    psum x1, waiting for transfers between devices, local(): lax.psum(partial_value.astype(jnp.bfloat16), 'head').astype(jnp.float32)  59.7 us
    all_gather x1, waiting for transfers between devices, local(): lax.all_gather(trunk_out, 'head', axis=2, tiled=True)  45.7 us
    unnamed x7, waiting for transfers between devices  40.6 us
    all_gather x1, waiting for transfers between devices, local(): lax.all_gather(pair_proj[:, :, C:].astype(jnp.bfloat16), 'ctx', axis=1, t...  36.8 us
    dot_general x8, matrix products, attend_block(): jnp.einsum('vhqk,vkhe->vhqe', weights.astype(jnp.bfloat16), value_rows, p...  19.3 us
    dot_general x8, matrix products, attend_block(): jnp.einsum('vqhe,vkhe->vhqk', queries, key_rows, preferred_element_type=j...  14.5 us
  transfers between devices with their start and end apart: 8, of which 8 were waited for; matrix products, arithmetic and copies ran while one was open for 2% of the time, Pallas kernels for 0%

commit v1 on v0

--- a/solution.py
+++ b/solution.py
@@ -1,14 +1,26 @@
+import functools
 import math
 import jax
 import jax.numpy as jnp
 from jax import lax
 from jax.sharding import PartitionSpec as P
+from jax.lax import all_to_all, psum
 
 HD = 128
 VD = 192
 C = 128
 NB = 16
 POOL = 4
+
+
+def node_spread(array_in, join_dim):
+    x_next = jnp.concatenate(
+        all_to_all(jnp.stack(psum(1, "ctx") * [array_in]), "ctx", 0, 0), join_dim
+    )
+    return x_next
+
+
+waves_perform = functools.partial(node_spread, join_dim=1)
 
 
 def extended(block, sides, width):
@@ -93,7 +105,7 @@
             jnp.zeros((variants, head_count, token_count, VD), jnp.float32),
         ),
         queries,
-        lax.all_gather(key_rows, "ctx", axis=1, tiled=True),
+        waves_perform(key_rows),
         lax.all_gather(value_rows, "ctx", axis=1, tiled=True),
     )
     row_max, row_sum, weighted = running

time: 488 us -> 454 us (0.930)
  waiting for transfers between devices: 359 us -> 311 us
  local copies, waits for them, and re-layouts: 23.6 us -> 30.7 us
  starting transfers between devices: 5.27 us -> 11.9 us
    all_gather x1 -> x0, waiting for transfers between devices: 71.1 us -> none  [local(): lax.all_gather(key_rows, 'ctx', axis=1, tiled=True)]
    all_to_all x0 -> x1, waiting for transfers between devices: none -> 56.4 us  [node_spread(): all_to_all(jnp.stack(psum(1, 'ctx') * [array_in]), 'ctx', 0, 0)]
    all_gather x1, waiting for transfers between devices: 93.5 us -> 60.9 us  [local(): lax.all_gather(value_rows, 'ctx', axis=1, tiled=True)]
    all_to_all x0 -> x1, starting transfers between devices: none -> 6.7 us  [node_spread(): all_to_all(jnp.stack(psum(1, 'ctx') * [array_in]), 'ctx', 0, 0)]
    unnamed x7 -> x6, waiting for transfers between devices: 40.6 us -> 40.6 us
  transfers between devices with their start and end apart: 8 -> 8, of which waited for: 8 -> 8; matrix products, arithmetic and copies ran while one was open for 2% -> 4% of each run, Pallas kernels for 0% -> 0%
where the time goes in v1:
time: 454 us; the launch traced here: 452 us
  waiting for transfers between devices  311 us (69%)
  matrix products  53.7 us (12%)
  local copies, waits for them, and re-layouts  30.7 us (7%)
  other arithmetic  30.4 us (7%)
  between operations  13.4 us (3%)
  starting transfers between devices  11.9 us (3%)
    all_gather x1, waiting for transfers between devices, local(): lax.all_gather(value_rows, 'ctx', axis=1, tiled=True)  60.9 us
    psum x1, waiting for transfers between devices, local(): lax.psum(partial_value.astype(jnp.bfloat16), 'head').astype(jnp.float32)  59.8 us
    all_to_all x1, waiting for transfers between devices, node_spread(): all_to_all(jnp.stack(psum(1, 'ctx') * [array_in]), 'ctx', 0, 0)  56.4 us
    all_gather x1, waiting for transfers between devices, local(): lax.all_gather(trunk_out, 'head', axis=2, tiled=True)  45.7 us
    unnamed x6, waiting for transfers between devices  40.6 us
    all_gather x1, waiting for transfers between devices, local(): lax.all_gather(pair_proj[:, :, C:].astype(jnp.bfloat16), 'ctx', axis=1, t...  36.8 us
    dot_general x8, matrix products, attend_block(): jnp.einsum('vhqk,vkhe->vhqe', weights.astype(jnp.bfloat16), value_rows, p...  19.4 us
    dot_general x8, matrix products, attend_block(): jnp.einsum('vqhe,vkhe->vhqk', queries, key_rows, preferred_element_type=j...  14.2 us
  transfers between devices with their start and end apart: 8, of which 8 were waited for; matrix products, arithmetic and copies ran while one was open for 4% of the time, Pallas kernels for 0%

profile of v1, /device:TPU:0, one launch (start us, length us, event | category | flops | bytes accessed | tf_op | source)
XLA Modules:
  0.0 451.9 jit_solution(16074030588416954691)
XLA Ops:
  7.4 1.0 broadcast_select_fusion
  8.5 3.6 collective-permute-start
  12.1 1.3 collective-permute-start.1
  13.4 7.0 %collective-permute-done = bf16[4,256,192]{1,2,0:T(8,128)(2,1)S(1)} collective-permute-done((bf16[4,256,192]{1,2,0:T(8,128)(2,1)S(1)}, bf16[4,256,192]{1,2,0:T(8,128)(2,1)S(1)}, u32[]{:S(2)}, u32[]{:S(2)}) %collective-permute-start) | collective-permute-done | bytes 393248 | tf_op jit(solution)/shard_map/ppermute | solution.py:31
  20.4 4.1 collective-permute-done.1
  25.0 1.8 copy-done.2
  26.8 2.0 fusion.28
  28.8 45.7 %all-gather.4.cloned.1.call-done = bf16[4,512,1536]{1,2,0:T(8,128)(2,1)} async-done(((bf16[4,512,192]{1,2,0:T(8,128)(2,1)}), bf16[4,512,1536]{1,2,0:T(8,128)(2,1)}) %all-gather.4.cloned.1.call-update) | async-done | bytes 6291472 | tf_op jit(solution)/shard_map/all_gather | solution.py:93
  74.5 5.8 %convert_bitcast_fusion = bf16[4,512,1,448]{1,3,0,2:T(8,128)(2,1)S(1)} fusion(bf16[4,512,1536]{1,2,0:T(8,128)(2,1)} %all-gather.4.cloned.1.call-done, bf16[1536,448]{0,1:T(8,128)(2,1)S(1)} %copy-done), kind=kOutput, calls=%fused_computation.29 | convolution fusion | flops 2819489792 | bytes 9502720 | tf_op jit(solution)/shard_map/vtd,df->vtf/dot_general | solution.py:91
  80.3 1.2 copy-done.4
  81.5 1.0 slice.81
  82.5 1.3 fusion.54
  84.1 3.0 stack.2
  87.1 6.7 %all-to-all-start = ((bf16[8,4,512,1,128]{4,2,1,3,0:T(8,128)(2,1)}), bf16[8,4,512,1,128]{4,2,1,3,0:T(8,128)(2,1)}, u32[]{:S(2)}, u32[]{:S(2)}) async-start(bf16[8,4,512,1,128]{4,2,1,3,0:T(8,128)(2,1)} %stack.2), calls=%async_computation | async-start | bytes 8388608 | tf_op jit(solution)/shard_map/all_to_all | solution.py:18
  94.1 56.4 %all-to-all-done = bf16[8,4,512,1,128]{4,2,1,3,0:T(8,128)(2,1)} async-done(((bf16[8,4,512,1,128]{4,2,1,3,0:T(8,128)(2,1)}), bf16[8,4,512,1,128]{4,2,1,3,0:T(8,128)(2,1)}, u32[]{:S(2)}, u32[]{:S(2)}) %all-to-all-start) | async-done | bytes 4194336 | tf_op jit(solution)/shard_map/all_to_all | solution.py:18
  150.5 4.7 %copy.38 = bf16[8,4,512,1,128]{4,2,0,1,3:T(8,128)(2,1)} copy(bf16[8,4,512,1,128]{4,2,1,3,0:T(8,128)(2,1)} %all-to-all-done) | data formatting | bytes 8388608 | tf_op jit(solution)/shard_map/all_to_all | solution.py:18
  155.2 60.9 %all-gather.6.cloned.1.call-done = bf16[4,4096,1,192]{1,3,0,2:T(8,128)(2,1)} async-done(((bf16[4,512,1,192]{1,3,0,2:T(8,128)(2,1)}), bf16[4,4096,1,192]{1,3,0,2:T(8,128)(2,1)}) %all-gather.6.cloned.1.call-update) | async-done | bytes 6291472 | tf_op jit(solution)/shard_map/all_gather | solution.py:109
  216.1 39.9 %while.18 = (s32[]{:T(128)}, f32[4,1,512]{2,0,1:T(4,128)S(1)}, f32[4,1,512]{2,0,1:T(4,128)S(1)}, f32[4,1,512,192]{2,3,0,1:T(8,128)S(1)}, bf16[4,4096,1,128]{3,1,...) while((s32[]{:T(128)}, f32[4,1,512]{2,0,1:T(4,128)S(1)}, ...), condition=%wide.region_3.4_spmd.clone, body=%wide.region_0.3_spmd.clone.sunk | while | flops 680669184 | bytes 17694904 | solution.py:67
  216.1 1.8 bitcast_reduce_fusion.3
  218.6 2.4 bitcast_add_fusion.5
  221.1 1.8 bitcast_reduce_fusion.3
  223.6 2.4 bitcast_add_fusion.5
  226.0 1.8 bitcast_reduce_fusion.3
  228.5 2.4 bitcast_add_fusion.5
  231.0 1.8 bitcast_reduce_fusion.3
  233.5 2.4 bitcast_add_fusion.5
  236.0 1.8 bitcast_reduce_fusion.3
  238.5 2.4 bitcast_add_fusion.5
  241.0 1.8 bitcast_reduce_fusion.3
  243.5 2.4 bitcast_add_fusion.5
  246.0 1.8 bitcast_reduce_fusion.3
  248.5 2.4 bitcast_add_fusion.5
  251.0 1.8 bitcast_reduce_fusion.3
  253.5 2.4 bitcast_add_fusion.5
  257.2 4.5 %fusion.19 = bf16[1536,2048]{0,1:T(8,128)(2,1)} fusion(bf16[2048,192]{0,1:T(8,128)(2,1)S(1)} %bitcast.99, bf16[192,1536]{1,0:T(8,128)(2,1)S(1)} %copy-done.5), kind=kOutput, calls=%fused_computation.26 | convolution fusion | flops 1211105280 | bytes 7667712 | tf_op jit(solution)/shard_map/dot_general | solution.py:115
  261.8 8.7 %copy.48 = bf16[1536,2048]{1,0:T(8,128)(2,1)} copy(bf16[1536,2048]{0,1:T(8,128)(2,1)} %fusion.19) | data formatting | bytes 12582912
  270.7 40.5 %reduce-scatter.4.cloned.1.call-done = bf16[192,2048]{1,0:T(8,128)(2,1)} async-done(((bf16[1536,2048]{1,0:T(8,128)(2,1)}), bf16[192,2048]{1,0:T(8,128)(2,1)}) %reduce-scatter.4.cloned.1.call-update) | async-done | bytes 786448
  311.3 1.4 copy.49
  312.7 1.5 reshape.224
  314.2 2.9 copy.42
  317.1 3.6 convert_add_fusion
  320.7 2.0 copy.43
  323.6 1.0 convolution_convert_fusion.1
  324.7 59.8 %all-reduce.2.cloned.1.call-done = bf16[4,128,256]{2,1,0:T(8,128)(2,1)} async-done(((bf16[4,128,256]{2,1,0:T(8,128)(2,1)}), bf16[4,128,256]{2,1,0:T(8,128)(2,1)}) %all-reduce.2.cloned.1.call-update) | async-done | bytes 262160 | tf_op jit(solution)/shard_map/psum | solution.py:131
  384.4 1.6 slice_convert_fusion
  386.3 8.9 %fusion.33 = f32[128,128,128]{2,1,0:T(8,128)} fusion(s32[128,128]{1,0:T(8,128)S(1)} %convert_add_fusion.1, f32[16,128]{1,0:T(8,128)S(1)} %copy-done.7), kind=kOutput, calls=%fused_computation.50 | convolution fusion | flops 402915328 | bytes 8462336 | tf_op jit(solution)/shard_map/dot_general | solution.py:148
  395.2 36.8 %all-gather.8.cloned.1.call-done = bf16[4,1024,128]{2,1,0:T(8,128)(2,1)} async-done(((bf16[4,128,128]{2,1,0:T(8,128)(2,1)}), bf16[4,1024,128]{2,1,0:T(8,128)(2,1)}) %all-gather.8.cloned.1.call-update) | async-done | bytes 1048592 | tf_op jit(solution)/shard_map/all_gather | solution.py:133
  433.0 12.4 %add_convert_fusion = bf16[4,128,128,128]{3,2,1,0:T(8,128)(2,1)} fusion(f32[128,128,128]{2,1,0:T(8,128)} %fusion.33, f32[4,128,128]{2,1,0:T(8,128)S(1)} %dynamic-slice_convert_fusion, f32[4,128,128]{2,1,0:T(8,128)S(1)} %get-tuple-element.213), kind=kLoop, calls=%fused_computation.24 | loop fusion | flops 25165824 | bytes 25690112 | tf_op jit(solution)/shard_map/convert_element_type | solution.py:150
  (79 shorter events, 11.5 us)
Async XLA Ops:
  6.5 68.0 %copy-start = (bf16[1536,448]{0,1:T(8,128)(2,1)S(1)}, bf16[1536,448]{0,1:T(8,128)(2,1)}, u32[]{:S(2)}) copy-start(bf16[1536,448]{0,1:T(8,128)(2,1)} %param.14) | copy-start | bytes 4128772
  6.5 6.9 %copy-start.9 = (f32[3,192]{1,0:T(4,128)S(1)}, f32[3,192]{1,0:T(4,128)}, u32[]{:S(2)}) copy-start(f32[3,192]{1,0:T(4,128)} %param.12) | copy-start | bytes 6916
  6.5 68.0 %all-gather.4.cloned.1.call-start = ((), (), s32[]{:S(2)}) async-start(), calls=%async_computation.2 | async-start | bytes 7077888 | tf_op jit(solution)/shard_map/all_gather | solution.py:93
  8.5 11.9 %collective-permute-start = (bf16[4,256,192]{1,2,0:T(8,128)(2,1)S(1)}, bf16[4,256,192]{1,2,0:T(8,128)(2,1)S(1)}, u32[]{:S(2)}, u32[]{:S(2)}) collective-permute-start(bf16[4,256,192]{1,2,0:T(8,128)(2,1)S(1)} %get-tuple-element.211), channel_id=1, source_target_pairs={{0,16},{16,32},{32,48},{48,64},{64,80},{80,96},{96,112},{1,17},{17... | collective-permute-start | bytes 1179656 | tf_op jit(solution)/shard_map/ppermute | solution.py:31
  12.1 12.5 %collective-permute-start.1 = (bf16[4,256,192]{1,2,0:T(8,128)(2,1)S(1)}, bf16[4,256,192]{1,2,0:T(8,128)(2,1)S(1)}, u32[]{:S(2)}, u32[]{:S(2)}) collective-permute-start(bf16[4,256,192]{1,2,0:T(8,128)(2,1)S(1)} %get-tuple-element.212), channel_id=1, source_target_pairs={{16,0},{32,16},{48,32},{64,48},{80,64},{96,80},{112,96},{17,1},{33... | collective-permute-start | bytes 1179656 | tf_op jit(solution)/shard_map/ppermute | solution.py:34
  13.4 13.4 %copy-start.8 = (f32[192]{0:T(256)S(1)}, f32[192]{0:T(256)}, u32[]{:S(2)}) copy-start(f32[192]{0:T(256)} %param.13) | copy-start | bytes 2308
  25.0 1.8 copy-start.2
  28.7 187.3 %all-gather.6.cloned.1.call-start = ((), (), s32[]{:S(2)}) async-start(), calls=%async_computation.3 | async-start | bytes 7077888 | tf_op jit(solution)/shard_map/all_gather | solution.py:109
  80.3 1.2 copy-start.4
  87.1 63.5 %all-to-all-start = ((bf16[8,4,512,1,128]{4,2,1,3,0:T(8,128)(2,1)}), bf16[8,4,512,1,128]{4,2,1,3,0:T(8,128)(2,1)}, u32[]{:S(2)}, u32[]{:S(2)}) async-start(bf16[8,4,512,1,128]{4,2,1,3,0:T(8,128)(2,1)} %stack.2), calls=%async_computation | async-start | bytes 8388608 | tf_op jit(solution)/shard_map/all_to_all | solution.py:18
  93.8 217.5 %reduce-scatter.4.cloned.1.call-start = ((), (), s32[]{:S(2)}) async-start(), calls=%async_computation.6 | async-start | bytes 7077888
  256.2 1.1 copy-start.5
  270.5 113.9 %all-reduce.2.cloned.1.call-start = ((), (), s32[]{:S(2)}) async-start(), calls=%async_computation.4 | async-start | bytes 524288 | tf_op jit(solution)/shard_map/psum | solution.py:131
  314.2 3.0 copy-start.3
  322.7 0.9 copy-start.6
  323.3 63.0 %copy-start.7 = (f32[16,128]{1,0:T(8,128)S(1)}, f32[16,128]{1,0:T(8,128)}, u32[]{:S(2)}) copy-start(f32[16,128]{1,0:T(8,128)} %param.17) | copy-start | bytes 24580
  324.6 107.4 %all-gather.8.cloned.1.call-start = ((), (), s32[]{:S(2)}) async-start(), calls=%async_computation.5 | async-start | bytes 1179648 | tf_op jit(solution)/shard_map/all_gather | solution.py:133
  433.0 12.4 %copy-start.1 = (bf16[1536,448]{0,1:T(8,128)(2,1)S(1)}, bf16[1536,448]{0,1:T(8,128)(2,1)}, u32[]{:S(2)}) copy-start(bf16[1536,448]{0,1:T(8,128)(2,1)} %param.14) | copy-start | bytes 4128772
Sparse Core Ops, SparseCore 0:
  28.9 45.5 all-gather.3
  82.6 133.4 all-gather.5
  270.6 40.5 reduce-scatter.3
  324.7 59.6 all-reduce.1
  386.8 45.1 all-gather.7
